TPU v7x, 128 devices: a whole 4x4x4 slice. The times are simulated.
128 devices in a mesh: dp: 8 (over y_lo, x), ctx: 16 (over z, y_hi, core).
Axes of the slice: x: 4, y: 4 (y_hi: 2, y_lo: 2; y = y_hi * 2 + y_lo), z: 4, core: 2. Of those that a mesh axis runs over, the one named last changes fastest.
Arguments:
- query_one: bfloat16 [16384, 4096], P(('dp', 'ctx')), parts along dimension 0, may hold values from -64 to 64
- query_two: bfloat16 [16384, 4096], P(('dp', 'ctx')), parts along dimension 0, may hold values from -64 to 64
- shared_keys: bfloat16 [16384, 512], P(('dp', 'ctx')), parts along dimension 0, may hold values from -8 to 8
- common_values: bfloat16 [16384, 512], P(('dp', 'ctx')), parts along dimension 0, may hold values from -6 to 6
- cotangent_one: bfloat16 [16384, 4096], P(('dp', 'ctx')), parts along dimension 0, may hold values from -96 to 96
- cotangent_two: bfloat16 [16384, 4096], P(('dp', 'ctx')), parts along dimension 0, may hold values from -96 to 96
- span_order: int32 [256], P('dp'), parts along dimension 0, may hold values from 0 to 31, each once
- lengths: int32 [64], P('dp'), parts along dimension 0, may hold values from 1 to 1024, 2048 in all
Outputs:
- query_grad_one: bfloat16 [16384, 4096], P(('dp', 'ctx')), parts along dimension 0
- query_grad_two: bfloat16 [16384, 4096], P(('dp', 'ctx')), parts along dimension 0
- key_grad: bfloat16 [16384, 512], P(('dp', 'ctx')), parts along dimension 0
- value_grad: bfloat16 [16384, 512], P(('dp', 'ctx')), parts along dimension 0
There are 8 independent parts, one for each index of `dp`. A program takes and returns all parts, laid end to end along the dimension named above; each array names one. Nothing has to cross between parts.
Inputs may be any that keep to these rules, and one draw needn't show every extreme that they name: `span_order`: a permutation. `lengths`: they sum to 2048; the largest is exactly 1024.
All inputs are finite; a program needn't handle non-finite values.
Results may differ from a plain program's by a relative error of at most 0.0075.
Values may be sent and summed in bfloat16 or wider, within the bound.
No kernel may reach another device: no remote copies, remote signals or barrier semaphores. Data moves between devices by JAX's collectives and lax.ppermute only.
A program may use at most 320 MiB of HBM per device.

v0:
```python
import jax
import jax.numpy as jnp
from jax import lax
from jax.sharding import PartitionSpec as P

HEAD_SIZE = 128
KEY_VALUE_HEADS = 4
QUERY_PER_KEY = 8
HALF = 64


def head_group(group_width, queries, key_rows, values, cotangent, visible):
    scale = HEAD_SIZE ** (-0.5)
    rows_here = queries.shape[0]
    query_block = queries[
        :, group_width * QUERY_PER_KEY * HEAD_SIZE : (group_width + 1) * QUERY_PER_KEY * HEAD_SIZE
    ].reshape(rows_here, QUERY_PER_KEY, HEAD_SIZE)
    cot_block = cotangent[
        :, group_width * QUERY_PER_KEY * HEAD_SIZE : (group_width + 1) * QUERY_PER_KEY * HEAD_SIZE
    ].reshape(rows_here, QUERY_PER_KEY, HEAD_SIZE)
    key_block = key_rows[:, group_width * HEAD_SIZE : (group_width + 1) * HEAD_SIZE]
    value_block = values[:, group_width * HEAD_SIZE : (group_width + 1) * HEAD_SIZE]
    scores = (
        jnp.einsum("thd,kd->htk", query_block, key_block, preferred_element_type=jnp.float32)
        * scale
    )
    scores = jnp.where(visible[None], scores, -1e30)
    peak = jnp.max(scores, axis=-1, keepdims=True)
    expo = jnp.exp(scores - peak)
    probs = expo / jnp.sum(expo, axis=-1, keepdims=True)
    probs_low = probs.astype(jnp.bfloat16)
    dprobs = jnp.einsum("thd,kd->htk", cot_block, value_block, preferred_element_type=jnp.float32)
    dsum = jnp.sum(probs * dprobs, axis=-1, keepdims=True)
    dscores_low = (probs * (dprobs - dsum) * scale).astype(jnp.bfloat16)
    query_part = jnp.einsum(
        "htk,kd->thd", dscores_low, key_block, preferred_element_type=jnp.float32
    ).reshape(rows_here, QUERY_PER_KEY * HEAD_SIZE)
    key_part = jnp.einsum(
        "htk,thd->kd", dscores_low, query_block, preferred_element_type=jnp.float32
    )
    value_part = jnp.einsum("htk,thd->kd", probs_low, cot_block, preferred_element_type=jnp.float32)
    return (query_part, key_part, value_part)


def layer_grads(queries, key_rows, values, cotangent, visible):
    query_parts, key_parts, value_parts = ([], [], [])
    for group_width in range(KEY_VALUE_HEADS):
        query_part, key_part, value_part = head_group(
            group_width, queries, key_rows, values, cotangent, visible
        )
        query_parts.append(query_part)
        key_parts.append(key_part)
        value_parts.append(value_part)
    return (
        jnp.concatenate(query_parts, axis=1),
        jnp.concatenate(key_parts, axis=1),
        jnp.concatenate(value_parts, axis=1),
    )


def local(
    query_one,
    query_two,
    shared_keys,
    common_values,
    cotangent_one,
    cotangent_two,
    span_order,
    lengths,
):
    all_keys, all_values = (
        lax.all_gather(shared_keys, "ctx", axis=0, tiled=True),
        lax.all_gather(common_values, "ctx", axis=0, tiled=True),
    )
    rows_here = query_one.shape[0]
    total_rows = all_keys.shape[0]
    device_index = lax.axis_index("ctx")
    rows = jnp.arange(total_rows, dtype=jnp.int32)
    slots = jnp.arange(span_order.shape[0], dtype=jnp.int32)
    one_hot = ((rows // HALF)[:, None] == slots[None, :]).astype(jnp.int32)
    positions = jnp.sum(one_hot * span_order[None, :], axis=1) * HALF + rows % HALF
    ends = jnp.cumsum(lengths)
    documents = jnp.sum((positions[:, None] >= ends[None, :]).astype(jnp.int32), axis=1)
    start_row = device_index * rows_here
    local_pos = lax.dynamic_slice_in_dim(positions, start_row, rows_here)
    local_doc = lax.dynamic_slice_in_dim(documents, start_row, rows_here)
    visible = (positions[None, :] <= local_pos[:, None]) & (
        documents[None, :] == local_doc[:, None]
    )
    grad_q1, grad_k1, grad_v1 = layer_grads(query_one, all_keys, all_values, cotangent_one, visible)
    grad_q2, grad_k2, grad_v2 = layer_grads(query_two, all_keys, all_values, cotangent_two, visible)
    width = grad_k1.shape[1]
    stacked = jnp.concatenate([grad_k1 + grad_k2, grad_v1 + grad_v2], axis=1)
    summed = lax.psum_scatter(stacked, "ctx", scatter_dimension=0, tiled=True)
    key_sum = summed[:, :width]
    value_sum = summed[:, width:]
    return (
        grad_q1.astype(jnp.bfloat16),
        grad_q2.astype(jnp.bfloat16),
        key_sum.astype(jnp.bfloat16),
        value_sum.astype(jnp.bfloat16),
    )


def solution(mesh):
    in_specs = (
        P(("dp", "ctx"), None),
        P(("dp", "ctx"), None),
        P(("dp", "ctx"), None),
        P(("dp", "ctx"), None),
        P(("dp", "ctx"), None),
        P(("dp", "ctx"), None),
        P("dp"),
        P("dp"),
    )
    out_specs = (
        P(("dp", "ctx"), None),
        P(("dp", "ctx"), None),
        P(("dp", "ctx"), None),
        P(("dp", "ctx"), None),
    )
    return jax.shard_map(local, mesh=mesh, in_specs=in_specs, out_specs=out_specs, check_vma=False)
```

profile of v0, /device:TPU:1, one launch (start us, length us, event | category | flops | bytes accessed | tf_op | source)
XLA Modules:
  0.0 492.2 jit_solution(15425951806183071014)
XLA Ops:
  24.2 37.6 %all-gather.3.cloned.1.call-done = bf16[2048,512]{1,0:T(8,128)(2,1)} async-done(((bf16[128,512]{1,0:T(8,128)(2,1)}), bf16[2048,512]{1,0:T(8,128)(2,1)}) %all-gather.3.cloned.1.call-update) | async-done | bytes 2097168 | tf_op jit(solution)/shard_map/all_gather | solution.py:72
  61.8 7.1 %fusion.241 = (f32[8,128]{1,0:T(8,128)S(1)}, f32[8,128,2048]{1,2,0:T(8,128)}) fusion(pred[128,2048]{0,1:T(8,128)(4,1)S(1)} %compare_and_fusion, bf16[128,8,128]{0,2,1:T(8,128)(2,1)} %bitcast.560, bf16[2048,512]{1,0:T(8,128)(2,1)} %all-gather.3.cloned.1.call-done), kind=kOutput, calls=%fused_computation.278 | convolution fusion | flops 545261568 | bytes 9441280 | tf_op jit(solution)/shard_map/sub | solution.py:29
  68.9 5.9 %fusion.141 = f32[2048,128]{0,1:T(8,128)} fusion(bf16[128,8,128]{0,2,1:T(8,128)(2,1)S(1)} %bitcast.544, f32[8,128,2048]{1,2,0:T(8,128)} %get-tuple-element.43, f32[8,128]{1,0:T(8,128)S(1)} %get-tuple-element.42), kind=kOutput, calls=%fused_computation.170 | convolution fusion | flops 541065216 | bytes 9703424 | tf_op jit(solution)/shard_map/htk,thd->kd/dot_general | solution.py:41
  74.8 35.8 %all-gather.5.cloned.1.call-done = bf16[2048,512]{1,0:T(8,128)(2,1)} async-done(((bf16[128,512]{1,0:T(8,128)(2,1)}), bf16[2048,512]{1,0:T(8,128)(2,1)}) %all-gather.5.cloned.1.call-update) | async-done | bytes 2097168 | tf_op jit(solution)/shard_map/all_gather | solution.py:73
  116.1 14.5 %fusion.112 = f32[2048,128]{0,1:T(8,128)} fusion(bf16[128,8,128]{0,2,1:T(8,128)(2,1)S(1)} %bitcast.561, f32[2048,128,8]{1,0,2:T(8,128)} %fusion.174, f32[8,128,2048]{1,2,0:T(8,128)} %get-tuple-element.43, f32[8,128]{1,0:T(8,128)S(1)} %get-tuple-element.42), kind=kOutput, calls=%fused_computation.155 | convolution fusion | flops 551554048 | bytes 18092032 | tf_op jit(solution)/shard_map/htk,thd->kd/dot_general | solution.py:38
  130.6 7.0 %fusion.243 = (f32[8,128]{1,0:T(8,128)S(1)}, f32[8,128,2048]{1,2,0:T(8,128)}) fusion(pred[128,2048]{0,1:T(8,128)(4,1)S(1)} %compare_and_fusion, bf16[128,8,128]{0,2,1:T(8,128)(2,1)S(1)} %bitcast.559, bf16[2048,512]{1,0:T(8,128)(2,1)} %all-gather.3.cloned.1.call-done), kind=kOutput, calls=%fused_computation.280 | convolution fusion | flops 545261568 | bytes 9441280 | tf_op jit(solution)/shard_map/sub | solution.py:29
  137.7 6.0 %fusion.135 = f32[2048,128]{0,1:T(8,128)} fusion(bf16[128,8,128]{0,2,1:T(8,128)(2,1)S(1)} %bitcast.542, f32[8,128,2048]{1,2,0:T(8,128)} %get-tuple-element.47, f32[8,128]{1,0:T(8,128)S(1)} %get-tuple-element.46), kind=kOutput, calls=%fused_computation.168 | convolution fusion | flops 541065216 | bytes 9703424 | tf_op jit(solution)/shard_map/htk,thd->kd/dot_general | solution.py:41
  148.1 14.2 %fusion.114 = f32[2048,128]{0,1:T(8,128)} fusion(bf16[128,8,128]{0,2,1:T(8,128)(2,1)} %bitcast.558, f32[2048,128,8]{1,0,2:T(8,128)} %fusion.170, f32[8,128,2048]{1,2,0:T(8,128)} %get-tuple-element.47, f32[8,128]{1,0:T(8,128)S(1)} %get-tuple-element.46), kind=kOutput, calls=%fused_computation.157 | convolution fusion | flops 551554048 | bytes 18092032 | tf_op jit(solution)/shard_map/htk,thd->kd/dot_general | solution.py:38
  162.3 7.1 %fusion.242 = (f32[8,128]{1,0:T(8,128)S(1)}, f32[8,128,2048]{1,2,0:T(8,128)}) fusion(pred[128,2048]{0,1:T(8,128)(4,1)S(1)} %copy-done.13, bf16[128,8,128]{0,2,1:T(8,128)(2,1)} %bitcast.556, bf16[2048,512]{1,0:T(8,128)(2,1)} %all-gather.3.cloned.1.call-done), kind=kOutput, calls=%fused_computation.279 | convolution fusion | flops 545261568 | bytes 9441280 | tf_op jit(solution)/shard_map/sub | solution.py:29
  179.9 14.2 %fusion.113 = f32[2048,128]{0,1:T(8,128)} fusion(bf16[128,8,128]{0,2,1:T(8,128)(2,1)} %bitcast.557, f32[2048,128,8]{1,0,2:T(8,128)} %fusion.172, f32[8,128,2048]{1,2,0:T(8,128)} %get-tuple-element.45, f32[8,128]{1,0:T(8,128)S(1)} %get-tuple-element.44), kind=kOutput, calls=%fused_computation.156 | convolution fusion | flops 551554048 | bytes 18092032 | tf_op jit(solution)/shard_map/htk,thd->kd/dot_general | solution.py:38
  194.1 7.0 %fusion.244 = (f32[8,128]{1,0:T(8,128)S(1)}, f32[8,128,2048]{1,2,0:T(8,128)}) fusion(pred[128,2048]{0,1:T(8,128)(4,1)S(1)} %copy-done.13, bf16[128,8,128]{0,2,1:T(8,128)(2,1)S(1)} %bitcast.554, bf16[2048,512]{1,0:T(8,128)(2,1)} %all-gather.3.cloned.1.call-done), kind=kOutput, calls=%fused_computation.281 | convolution fusion | flops 545261568 | bytes 9441280 | tf_op jit(solution)/shard_map/sub | solution.py:29
  201.1 5.9 %fusion.132 = f32[2048,128]{0,1:T(8,128)} fusion(bf16[128,8,128]{0,2,1:T(8,128)(2,1)S(1)} %bitcast.538, f32[8,128,2048]{1,2,0:T(8,128)} %get-tuple-element.49, f32[8,128]{1,0:T(8,128)S(1)} %get-tuple-element.48), kind=kOutput, calls=%fused_computation.167 | convolution fusion | flops 541065216 | bytes 9703424 | tf_op jit(solution)/shard_map/htk,thd->kd/dot_general | solution.py:41
  211.5 14.8 %fusion.115 = f32[2048,128]{0,1:T(8,128)} fusion(bf16[128,8,128]{0,2,1:T(8,128)(2,1)S(1)} %bitcast.555, f32[2048,128,8]{1,0,2:T(8,128)} %fusion.168, f32[8,128,2048]{1,2,0:T(8,128)} %get-tuple-element.49, f32[8,128]{1,0:T(8,128)S(1)} %get-tuple-element.48), kind=kOutput, calls=%fused_computation.158 | convolution fusion | flops 551554048 | bytes 18092032 | tf_op jit(solution)/shard_map/htk,thd->kd/dot_general | solution.py:38
  226.3 7.0 %fusion.237 = (f32[8,128]{1,0:T(8,128)S(1)}, f32[8,128,2048]{1,2,0:T(8,128)}) fusion(pred[128,2048]{0,1:T(8,128)(4,1)S(1)} %copy-done.13, bf16[128,8,128]{0,2,1:T(8,128)(2,1)S(1)} %bitcast.552, bf16[2048,512]{1,0:T(8,128)(2,1)} %all-gather.3.cloned.1.call-done), kind=kOutput, calls=%fused_computation.274 | convolution fusion | flops 545261568 | bytes 9441280 | tf_op jit(solution)/shard_map/sub | solution.py:29
  243.6 14.4 %fusion.116 = f32[2048,128]{0,1:T(8,128)} fusion(bf16[128,8,128]{0,2,1:T(8,128)(2,1)S(1)} %bitcast.553, f32[2048,128,8]{1,0,2:T(8,128)} %fusion.175, f32[8,128,2048]{1,2,0:T(8,128)} %get-tuple-element.35, f32[8,128]{1,0:T(8,128)S(1)} %get-tuple-element.34), kind=kOutput, calls=%fused_computation.159 | convolution fusion | flops 551554048 | bytes 18092032 | tf_op jit(solution)/shard_map/htk,thd->kd/dot_general | solution.py:38
  258.0 7.0 %fusion.239 = (f32[8,128]{1,0:T(8,128)S(1)}, f32[8,128,2048]{1,2,0:T(8,128)}) fusion(pred[128,2048]{0,1:T(8,128)(4,1)S(1)} %copy-done.13, bf16[128,8,128]{0,2,1:T(8,128)(2,1)S(1)} %bitcast.550, bf16[2048,512]{1,0:T(8,128)(2,1)} %all-gather.3.cloned.1.call-done), kind=kOutput, calls=%fused_computation.276 | convolution fusion | flops 545261568 | bytes 9441280 | tf_op jit(solution)/shard_map/sub | solution.py:29
  275.5 14.6 %fusion.118 = f32[2048,128]{0,1:T(8,128)} fusion(bf16[128,8,128]{0,2,1:T(8,128)(2,1)S(1)} %bitcast.551, f32[2048,128,8]{1,0,2:T(8,128)} %fusion.171, f32[8,128,2048]{1,2,0:T(8,128)} %get-tuple-element.39, f32[8,128]{1,0:T(8,128)S(1)} %get-tuple-element.38), kind=kOutput, calls=%fused_computation.161 | convolution fusion | flops 551554048 | bytes 18092032 | tf_op jit(solution)/shard_map/htk,thd->kd/dot_general | solution.py:38
  290.0 7.1 %fusion.238 = (f32[8,128]{1,0:T(8,128)S(1)}, f32[8,128,2048]{1,2,0:T(8,128)}) fusion(pred[128,2048]{0,1:T(8,128)(4,1)S(1)} %copy-done.13, bf16[128,8,128]{0,2,1:T(8,128)(2,1)S(1)} %bitcast.548, bf16[2048,512]{1,0:T(8,128)(2,1)} %all-gather.3.cloned.1.call-done), kind=kOutput, calls=%fused_computation.275 | convolution fusion | flops 545261568 | bytes 9441280 | tf_op jit(solution)/shard_map/sub | solution.py:29
  297.2 5.9 %fusion.126 = f32[2048,128]{0,1:T(8,128)} fusion(bf16[128,8,128]{0,2,1:T(8,128)(2,1)S(1)} %bitcast.532, f32[8,128,2048]{1,2,0:T(8,128)} %get-tuple-element.37, f32[8,128]{1,0:T(8,128)S(1)} %get-tuple-element.36), kind=kOutput, calls=%fused_computation.165 | convolution fusion | flops 541065216 | bytes 9703424 | tf_op jit(solution)/shard_map/htk,thd->kd/dot_general | solution.py:41
  307.5 14.3 %fusion.117 = f32[2048,128]{0,1:T(8,128)} fusion(bf16[128,8,128]{0,2,1:T(8,128)(2,1)S(1)} %bitcast.549, f32[2048,128,8]{1,0,2:T(8,128)} %fusion.173, f32[8,128,2048]{1,2,0:T(8,128)} %get-tuple-element.37, f32[8,128]{1,0:T(8,128)S(1)} %get-tuple-element.36), kind=kOutput, calls=%fused_computation.160 | convolution fusion | flops 551554048 | bytes 18092032 | tf_op jit(solution)/shard_map/htk,thd->kd/dot_general | solution.py:38
  321.9 7.1 %fusion.240 = (f32[8,128]{1,0:T(8,128)S(1)}, f32[8,128,2048]{1,2,0:T(8,128)}) fusion(pred[128,2048]{0,1:T(8,128)(4,1)S(1)} %copy-done.14, bf16[128,8,128]{0,2,1:T(8,128)(2,1)S(1)} %bitcast.546, bf16[2048,512]{1,0:T(8,128)(2,1)} %all-gather.3.cloned.1.call-done), kind=kOutput, calls=%fused_computation.277 | convolution fusion | flops 545261568 | bytes 9441280 | tf_op jit(solution)/shard_map/sub | solution.py:29
  339.3 14.4 %fusion.119 = f32[2048,128]{0,1:T(8,128)} fusion(bf16[128,8,128]{0,2,1:T(8,128)(2,1)S(1)} %bitcast.547, f32[2048,128,8]{1,0,2:T(8,128)} %fusion.169, f32[8,128,2048]{1,2,0:T(8,128)} %get-tuple-element.41, f32[8,128]{1,0:T(8,128)S(1)} %get-tuple-element.40), kind=kOutput, calls=%fused_computation.162 | convolution fusion | flops 551554048 | bytes 18092032 | tf_op jit(solution)/shard_map/htk,thd->kd/dot_general | solution.py:38
  353.7 8.1 %maximum_add_fusion = (f32[2048,512]{0,1:T(8,128)S(1)}, f32[2048,512]{0,1:T(8,128)}) fusion(f32[2048,128]{0,1:T(8,128)} %fusion.116, f32[2048,128]{0,1:T(8,128)} %fusion.117, f32[2048,128]{0,1:T(8,128)} %fusion.118, f32[2048,128]{0,1:T(8,128)} %fusion.119, f32[2048,128]{0,1:T(8,128)S(1)} %copy-done.5, f32[2048,128]{0,1:T(8,128)} %fusion.113, ...), kind=kLoop, calls=%fused_computation.81 | loop fusion | flops 14680064 | bytes 25165824 | tf_op jit(solution)/shard_map/add | solution.py:93
  361.8 6.5 %pad_maximum_fusion = f32[2048,1024]{0,1:T(8,128)} fusion(f32[2048,512]{0,1:T(8,128)} %get-tuple-element.51, f32[2048,512]{0,1:T(8,128)S(1)} %get-tuple-element.50), kind=kLoop, calls=%fused_computation.16 | loop fusion | flops 2097152 | bytes 16777216 | tf_op jit(solution)/shard_map/concatenate | solution.py:93
  369.9 14.6 %fusion.144 = bf16[8,128,128]{1,2,0:T(8,128)(2,1)S(1)} fusion(f32[2048,128,8]{1,0,2:T(8,128)} %fusion.174, bf16[2048,512]{1,0:T(8,128)(2,1)S(1)} %copy-done.17, f32[8,128,2048]{1,2,0:T(8,128)} %get-tuple-element.43, f32[8,128]{1,0:T(8,128)S(1)} %copy-done.19), kind=kOutput, calls=%fused_computation.171 | convolution fusion | flops 551685120 | bytes 34349056 | tf_op jit(solution)/shard_map/htk,kd->thd/dot_general | solution.py:35
  384.7 14.8 %fusion.146 = bf16[8,128,128]{1,2,0:T(8,128)(2,1)S(1)} fusion(f32[2048,128,8]{1,0,2:T(8,128)} %fusion.170, bf16[2048,512]{1,0:T(8,128)(2,1)S(1)} %copy-done.17, f32[8,128,2048]{1,2,0:T(8,128)} %get-tuple-element.47, f32[8,128]{1,0:T(8,128)S(1)} %copy-done.21), kind=kOutput, calls=%fused_computation.173 | convolution fusion | flops 551685120 | bytes 34349056 | tf_op jit(solution)/shard_map/htk,kd->thd/dot_general | solution.py:35
  399.7 13.8 %fusion.145 = bf16[8,128,128]{1,2,0:T(8,128)(2,1)S(1)} fusion(f32[2048,128,8]{1,0,2:T(8,128)} %fusion.172, bf16[2048,512]{1,0:T(8,128)(2,1)S(1)} %copy-done.17, f32[8,128,2048]{1,2,0:T(8,128)} %get-tuple-element.45, f32[8,128]{1,0:T(8,128)S(1)} %copy-done.23), kind=kOutput, calls=%fused_computation.172 | convolution fusion | flops 551685120 | bytes 34349056 | tf_op jit(solution)/shard_map/htk,kd->thd/dot_general | solution.py:35
  413.7 13.5 %fusion.147 = bf16[8,128,128]{1,2,0:T(8,128)(2,1)S(1)} fusion(f32[2048,128,8]{1,0,2:T(8,128)} %fusion.168, bf16[2048,512]{1,0:T(8,128)(2,1)S(1)} %copy-done.17, f32[8,128,2048]{1,2,0:T(8,128)} %get-tuple-element.49, f32[8,128]{1,0:T(8,128)S(1)} %copy-done.25), kind=kOutput, calls=%fused_computation.174 | convolution fusion | flops 551685120 | bytes 34349056 | tf_op jit(solution)/shard_map/htk,kd->thd/dot_general | solution.py:35
  427.3 13.5 %fusion.148 = bf16[8,128,128]{1,2,0:T(8,128)(2,1)S(1)} fusion(f32[2048,128,8]{1,0,2:T(8,128)} %fusion.175, bf16[2048,512]{1,0:T(8,128)(2,1)} %all-gather.3.cloned.1.call-done, f32[8,128,2048]{1,2,0:T(8,128)} %get-tuple-element.35, f32[8,128]{1,0:T(8,128)S(1)} %copy-done.27), kind=kOutput, calls=%fused_computation.175 | convolution fusion | flops 551685120 | bytes 34349056 | tf_op jit(solution)/shard_map/htk,kd->thd/dot_general | solution.py:35
  441.0 13.4 %fusion.150 = bf16[8,128,128]{1,2,0:T(8,128)(2,1)S(1)} fusion(f32[2048,128,8]{1,0,2:T(8,128)} %fusion.171, bf16[2048,512]{1,0:T(8,128)(2,1)} %all-gather.3.cloned.1.call-done, f32[8,128,2048]{1,2,0:T(8,128)} %get-tuple-element.39, f32[8,128]{1,0:T(8,128)S(1)} %get-tuple-element.38), kind=kOutput, calls=%fused_computation.177 | convolution fusion | flops 551685120 | bytes 34349056 | tf_op jit(solution)/shard_map/htk,kd->thd/dot_general | solution.py:35
  454.6 13.4 %fusion.149 = bf16[8,128,128]{1,2,0:T(8,128)(2,1)S(1)} fusion(f32[2048,128,8]{1,0,2:T(8,128)} %fusion.173, bf16[2048,512]{1,0:T(8,128)(2,1)} %all-gather.3.cloned.1.call-done, f32[8,128,2048]{1,2,0:T(8,128)} %get-tuple-element.37, f32[8,128]{1,0:T(8,128)S(1)} %get-tuple-element.36), kind=kOutput, calls=%fused_computation.176 | convolution fusion | flops 551685120 | bytes 34349056 | tf_op jit(solution)/shard_map/htk,kd->thd/dot_general | solution.py:35
  468.1 13.1 %fusion.151 = bf16[8,128,128]{1,2,0:T(8,128)(2,1)S(1)} fusion(f32[2048,128,8]{1,0,2:T(8,128)} %fusion.169, bf16[2048,512]{1,0:T(8,128)(2,1)} %all-gather.3.cloned.1.call-done, f32[8,128,2048]{1,2,0:T(8,128)} %get-tuple-element.41, f32[8,128]{1,0:T(8,128)S(1)} %get-tuple-element.40), kind=kOutput, calls=%fused_computation.178 | convolution fusion | flops 551685120 | bytes 34349056 | tf_op jit(solution)/shard_map/htk,kd->thd/dot_general | solution.py:35
  (116 shorter events, 84.2 us)
Async XLA Ops:
  7.2 12.1 %copy-start.6 = (bf16[128,4096]{1,0:T(8,128)(2,1)S(1)}, bf16[128,4096]{1,0:T(8,128)(2,1)}, u32[]{:S(2)}) copy-start(bf16[128,4096]{1,0:T(8,128)(2,1)} %param.12) | copy-start | bytes 3145732
  7.2 14.9 %copy-start.7 = (bf16[128,4096]{1,0:T(8,128)(2,1)S(1)}, bf16[128,4096]{1,0:T(8,128)(2,1)}, u32[]{:S(2)}) copy-start(bf16[128,4096]{1,0:T(8,128)(2,1)} %param.13) | copy-start | bytes 3145732
  7.2 54.6 %all-gather.3.cloned.1.call-start = ((), (), s32[]{:S(2)}) async-start(), calls=%async_computation.1 | async-start | bytes 2228224 | tf_op jit(solution)/shard_map/all_gather | solution.py:72
  7.9 102.7 %all-gather.5.cloned.1.call-start = ((), (), s32[]{:S(2)}) async-start(), calls=%async_computation.2 | async-start | bytes 2228224 | tf_op jit(solution)/shard_map/all_gather | solution.py:73
  8.7 474.2 %reduce-scatter.2.cloned.1.call-start = ((), (), s32[]{:S(2)}) async-start(), calls=%async_computation.3 | async-start | bytes 8912896 | tf_op jit(solution)/shard_map/reduce_scatter | solution.py:94
  24.2 106.4 %copy-start.12 = (pred[128,2048]{0,1:T(8,128)(4,1)}, pred[128,2048]{0,1:T(8,128)(4,1)S(1)}, u32[]{:S(2)}) copy-start(pred[128,2048]{0,1:T(8,128)(4,1)S(1)} %compare_and_fusion) | copy-start | bytes 786436
  68.9 47.2 %copy-start.18 = (f32[8,128]{1,0:T(8,128)}, f32[8,128]{1,0:T(8,128)S(1)}, u32[]{:S(2)}) copy-start(f32[8,128]{1,0:T(8,128)S(1)} %get-tuple-element.42) | copy-start | bytes 12292
  74.8 41.3 %copy-start.16 = (bf16[128,1024]{0,1:T(8,128)(2,1)S(1)}, bf16[128,1024]{0,1:T(8,128)(2,1)}, u32[]{:S(2)}) copy-start(bf16[128,1024]{0,1:T(8,128)(2,1)} %copy.288) | copy-start | bytes 786436
  116.1 14.5 %copy-start.15 = (bf16[128,1024]{0,1:T(8,128)(2,1)S(1)}, bf16[128,1024]{0,1:T(8,128)(2,1)}, u32[]{:S(2)}) copy-start(bf16[128,1024]{0,1:T(8,128)(2,1)} %copy.284) | copy-start | bytes 786436
  137.7 10.5 %copy-start.20 = (f32[8,128]{1,0:T(8,128)}, f32[8,128]{1,0:T(8,128)S(1)}, u32[]{:S(2)}) copy-start(f32[8,128]{1,0:T(8,128)S(1)} %get-tuple-element.46) | copy-start | bytes 12292
  137.7 6.0 %copy-start = (bf16[2048,512]{1,0:T(8,128)(2,1)S(1)}, bf16[2048,512]{1,0:T(8,128)(2,1)}, u32[]{:S(2)}) copy-start(bf16[2048,512]{1,0:T(8,128)(2,1)} %all-gather.5.cloned.1.call-done) | copy-start | bytes 6291460
  148.1 14.2 %copy-start.13 = (pred[128,2048]{0,1:T(8,128)(4,1)S(1)}, pred[128,2048]{0,1:T(8,128)(4,1)}, u32[]{:S(2)}) copy-start(pred[128,2048]{0,1:T(8,128)(4,1)} %copy-done.12) | copy-start | bytes 786436
  169.4 10.5 %copy-start.22 = (f32[8,128]{1,0:T(8,128)}, f32[8,128]{1,0:T(8,128)S(1)}, u32[]{:S(2)}) copy-start(f32[8,128]{1,0:T(8,128)S(1)} %get-tuple-element.44) | copy-start | bytes 12292
  179.9 14.2 %copy-start.11 = (bf16[128,1024]{0,1:T(8,128)(2,1)S(1)}, bf16[128,1024]{0,1:T(8,128)(2,1)}, u32[]{:S(2)}) copy-start(bf16[128,1024]{0,1:T(8,128)(2,1)} %copy.282) | copy-start | bytes 786436
  201.1 10.3 %copy-start.24 = (f32[8,128]{1,0:T(8,128)}, f32[8,128]{1,0:T(8,128)S(1)}, u32[]{:S(2)}) copy-start(f32[8,128]{1,0:T(8,128)S(1)} %get-tuple-element.48) | copy-start | bytes 12292
  233.2 10.4 %copy-start.26 = (f32[8,128]{1,0:T(8,128)}, f32[8,128]{1,0:T(8,128)S(1)}, u32[]{:S(2)}) copy-start(f32[8,128]{1,0:T(8,128)S(1)} %get-tuple-element.34) | copy-start | bytes 12292
  243.6 14.4 %copy-start.10 = (bf16[128,1024]{0,1:T(8,128)(2,1)S(1)}, bf16[128,1024]{0,1:T(8,128)(2,1)}, u32[]{:S(2)}) copy-start(bf16[128,1024]{0,1:T(8,128)(2,1)} %copy.276) | copy-start | bytes 786436
  258.0 7.0 %copy-start.3 = (bf16[128,1024]{0,1:T(8,128)(2,1)S(1)}, bf16[128,1024]{0,1:T(8,128)(2,1)}, u32[]{:S(2)}) copy-start(bf16[128,1024]{0,1:T(8,128)(2,1)} %copy.277) | copy-start | bytes 786436
  275.5 14.6 %copy-start.9 = (bf16[128,1024]{0,1:T(8,128)(2,1)S(1)}, bf16[128,1024]{0,1:T(8,128)(2,1)}, u32[]{:S(2)}) copy-start(bf16[128,1024]{0,1:T(8,128)(2,1)} %copy.278) | copy-start | bytes 786436
  290.0 7.1 %copy-start.2 = (bf16[128,1024]{0,1:T(8,128)(2,1)S(1)}, bf16[128,1024]{0,1:T(8,128)(2,1)}, u32[]{:S(2)}) copy-start(bf16[128,1024]{0,1:T(8,128)(2,1)} %copy.279) | copy-start | bytes 786436
  307.5 14.3 %copy-start.8 = (bf16[128,1024]{0,1:T(8,128)(2,1)S(1)}, bf16[128,1024]{0,1:T(8,128)(2,1)}, u32[]{:S(2)}) copy-start(bf16[128,1024]{0,1:T(8,128)(2,1)} %copy.274) | copy-start | bytes 786436
  307.5 14.3 %copy-start.14 = (pred[128,2048]{0,1:T(8,128)(4,1)S(1)}, pred[128,2048]{0,1:T(8,128)(4,1)}, u32[]{:S(2)}) copy-start(pred[128,2048]{0,1:T(8,128)(4,1)} %copy-done.12) | copy-start | bytes 786436
  321.9 7.1 %copy-start.1 = (bf16[128,1024]{0,1:T(8,128)(2,1)S(1)}, bf16[128,1024]{0,1:T(8,128)(2,1)}, u32[]{:S(2)}) copy-start(bf16[128,1024]{0,1:T(8,128)(2,1)} %copy.275) | copy-start | bytes 786436
  339.3 14.4 %copy-start.4 = (f32[2048,128]{0,1:T(8,128)S(1)}, f32[2048,128]{0,1:T(8,128)}, u32[]{:S(2)}) copy-start(f32[2048,128]{0,1:T(8,128)} %fusion.141) | copy-start | bytes 3145732
  339.3 14.4 %copy-start.5 = (f32[2048,128]{0,1:T(8,128)S(1)}, f32[2048,128]{0,1:T(8,128)}, u32[]{:S(2)}) copy-start(f32[2048,128]{0,1:T(8,128)} %fusion.112) | copy-start | bytes 3145732
  368.3 1.6 copy-start.17
  368.3 1.6 copy-start.19
  369.9 14.8 %copy-start.21 = (f32[8,128]{1,0:T(8,128)S(1)}, f32[8,128]{1,0:T(8,128)}, u32[]{:S(2)}) copy-start(f32[8,128]{1,0:T(8,128)} %copy-done.20) | copy-start | bytes 12292
  384.7 15.0 %copy-start.23 = (f32[8,128]{1,0:T(8,128)S(1)}, f32[8,128]{1,0:T(8,128)}, u32[]{:S(2)}) copy-start(f32[8,128]{1,0:T(8,128)} %copy-done.22) | copy-start | bytes 12292
  399.7 13.9 %copy-start.25 = (f32[8,128]{1,0:T(8,128)S(1)}, f32[8,128]{1,0:T(8,128)}, u32[]{:S(2)}) copy-start(f32[8,128]{1,0:T(8,128)} %copy-done.24) | copy-start | bytes 12292
  413.6 13.6 %copy-start.27 = (f32[8,128]{1,0:T(8,128)S(1)}, f32[8,128]{1,0:T(8,128)}, u32[]{:S(2)}) copy-start(f32[8,128]{1,0:T(8,128)} %copy-done.26) | copy-start | bytes 12292
Sparse Core Ops, SparseCore 0:
  10.5 51.2 all-gather.2
  64.3 46.3 all-gather.4
  368.5 99.8 reduce-scatter.1
where the time goes:
time: 500 us; the launch traced here: 492 us
  matrix products  366 us (73%)
  waiting for transfers between devices  74.8 us (15%)
  other arithmetic  20.2 us (4%)
  local copies, waits for them, and re-layouts  16.7 us (3%)
  between operations  14.3 us (3%)
    dot_general x8, matrix products, head_group(): jnp.einsum('htk,thd->kd', dscores_low, query_block, preferred_element_typ...  115 us
    dot_general x8, matrix products, head_group(): jnp.einsum('htk,kd->thd', dscores_low, key_block, preferred_element_type=...  110 us
    sub x8, matrix products, head_group(): expo = jnp.exp(scores - peak)  56.5 us
    dot_general x8, matrix products, head_group(): jnp.einsum('htk,thd->kd', probs_low, cot_block, preferred_element_type=jn...  47.3 us
    all_gather x1, waiting for transfers between devices, local(): lax.all_gather(shared_keys, 'ctx', axis=0, tiled=True)  37.6 us
    dot_general x8, matrix products, head_group(): jnp.einsum('thd,kd->htk', cot_block, value_block, preferred_element_type=...  36.9 us
    all_gather x1, waiting for transfers between devices, local(): lax.all_gather(common_values, 'ctx', axis=0, tiled=True)  35.8 us
    unnamed x74, local copies, waits for them, and re-layouts  12.7 us
  transfers between devices with their start and end apart: 3, of which 2 were waited for; matrix products, arithmetic and copies ran while one was open for 29% of the time, Pallas kernels for 0%

commit v1 on v0

--- a/solution.py
+++ b/solution.py
@@ -68,8 +68,11 @@
     span_order,
     lengths,
 ):
+    plan_core = lambda arr_in: jnp.concatenate(
+        lax.all_to_all(jnp.stack([arr_in] * lax.axis_size("ctx"), axis=0), "ctx", 0, 0), axis=0
+    )
     all_keys, all_values = (
-        lax.all_gather(shared_keys, "ctx", axis=0, tiled=True),
+        plan_core(shared_keys),
         lax.all_gather(common_values, "ctx", axis=0, tiled=True),
     )
     rows_here = query_one.shape[0]

time: 500 us -> 441 us (0.88)
  waiting for transfers between devices: 74.8 us -> 0.7 us
  local copies, waits for them, and re-layouts: 16.7 us -> 38.7 us
  matrix products: 366 us -> 352 us
  starting transfers between devices: 0.11 us -> 9.55 us
    all_gather x1 -> x0, waiting for transfers between devices: 37.6 us -> none  [local(): lax.all_gather(shared_keys, 'ctx', axis=0, tiled=True)]
    all_gather x1, waiting for transfers between devices: 35.8 us -> 0.01 us  [local(): lax.all_gather(common_values, 'ctx', axis=0, tiled=True)]
    dot_general x8, matrix products: 47.3 us -> 30.6 us  [head_group(): jnp.einsum('htk,thd->kd', probs_low, cot_block, preferred_element_type=jn...]
    unnamed x74 -> x68, local copies, waits for them, and re-layouts: 12.7 us -> 23.4 us
    all_to_all x0 -> x1, starting transfers between devices: none -> 9.47 us  [local(): lax.all_to_all(jnp.stack([arr_in] * lax.axis_size('ctx'), axis=0), 'ctx',...]
    reshape x8, local copies, waits for them, and re-layouts: 1.16 us -> 6.32 us  [head_group(): query_part = jnp.einsum('htk,kd->thd', dscores_low, key_block, preferred_...]
  transfers between devices with their start and end apart: 3 -> 3, of which waited for: 2 -> 0; matrix products, arithmetic and copies ran while one was open for 29% -> 55% of each run, Pallas kernels for 0% -> 0%
where the time goes in v1:
time: 441 us; the launch traced here: 437 us
  matrix products  352 us (80%)
  local copies, waits for them, and re-layouts  38.7 us (9%)
  other arithmetic  22.3 us (5%)
  between operations  14.5 us (3%)
  starting transfers between devices  9.55 us (2%)
    dot_general x8, matrix products, head_group(): jnp.einsum('htk,thd->kd', dscores_low, query_block, preferred_element_typ...  114 us
    dot_general x8, matrix products, head_group(): jnp.einsum('htk,kd->thd', dscores_low, key_block, preferred_element_type=...  113 us
    sub x8, matrix products, head_group(): expo = jnp.exp(scores - peak)  57.1 us
    dot_general x8, matrix products, head_group(): jnp.einsum('thd,kd->htk', cot_block, value_block, preferred_element_type=...  36.8 us
    dot_general x8, matrix products, head_group(): jnp.einsum('htk,thd->kd', probs_low, cot_block, preferred_element_type=jn...  30.6 us
    unnamed x68, local copies, waits for them, and re-layouts  23.4 us
    all_to_all x1, starting transfers between devices, local(): lax.all_to_all(jnp.stack([arr_in] * lax.axis_size('ctx'), axis=0), 'ctx',...  9.47 us
  transfers between devices with their start and end apart: 3, of which 0 were waited for; matrix products, arithmetic and copies ran while one was open for 55% of the time, Pallas kernels for 0%

profile of v1, /device:TPU:1, one launch (start us, length us, event | category | flops | bytes accessed | tf_op | source)
XLA Modules:
  0.0 437.3 jit_solution(4462275549331445816)
XLA Ops:
  10.4 9.5 %all-to-all-start = ((bf16[16,128,512]{2,1,0:T(8,128)(2,1)}), bf16[16,128,512]{2,1,0:T(8,128)(2,1)S(1)}, u32[]{:S(2)}, u32[]{:S(2)}) async-start(bf16[16,128,512]{2,1,0:T(8,128)(2,1)} %stack.2), calls=%async_computation | async-start | bytes 4194304 | tf_op jit(solution)/shard_map/all_to_all | solution.py:72
  50.3 7.4 %fusion.242 = (f32[8,128]{1,0:T(8,128)S(1)}, f32[8,128,2048]{1,2,0:T(8,128)}) fusion(pred[128,2048]{0,1:T(8,128)(4,1)} %compare_and_fusion, bf16[128,8,128]{0,2,1:T(8,128)(2,1)} %bitcast.577, bf16[2048,512]{1,0:T(8,128)(2,1)S(1)} %bitcast.531), kind=kOutput, calls=%fused_computation.279 | convolution fusion | flops 545261568 | bytes 9441280 | tf_op jit(solution)/shard_map/sub | solution.py:29
  57.6 7.0 %fusion.238 = (f32[8,128]{1,0:T(8,128)S(1)}, f32[8,128,2048]{1,2,0:T(8,128)}) fusion(pred[128,2048]{0,1:T(8,128)(4,1)} %compare_and_fusion, bf16[128,8,128]{0,2,1:T(8,128)(2,1)} %bitcast.571, bf16[2048,512]{1,0:T(8,128)(2,1)S(1)} %bitcast.532), kind=kOutput, calls=%fused_computation.275 | convolution fusion | flops 545261568 | bytes 9441280 | tf_op jit(solution)/shard_map/sub | solution.py:29
  64.7 7.0 %fusion.243 = (f32[8,128]{1,0:T(8,128)S(1)}, f32[8,128,2048]{1,2,0:T(8,128)}) fusion(pred[128,2048]{0,1:T(8,128)(4,1)} %compare_and_fusion, bf16[128,8,128]{0,2,1:T(8,128)(2,1)} %bitcast.575, bf16[2048,512]{1,0:T(8,128)(2,1)S(1)} %bitcast.533), kind=kOutput, calls=%fused_computation.280 | convolution fusion | flops 545261568 | bytes 9441280 | tf_op jit(solution)/shard_map/sub | solution.py:29
  71.7 7.0 %fusion.239 = (f32[8,128]{1,0:T(8,128)S(1)}, f32[8,128,2048]{1,2,0:T(8,128)}) fusion(pred[128,2048]{0,1:T(8,128)(4,1)} %compare_and_fusion, bf16[128,8,128]{0,2,1:T(8,128)(2,1)} %bitcast.567, bf16[2048,512]{1,0:T(8,128)(2,1)S(1)} %bitcast.534), kind=kOutput, calls=%fused_computation.276 | convolution fusion | flops 545261568 | bytes 9441280 | tf_op jit(solution)/shard_map/sub | solution.py:29
  78.7 7.3 %fusion.241 = (f32[8,128]{1,0:T(8,128)S(1)}, f32[8,128,2048]{1,2,0:T(8,128)}) fusion(pred[128,2048]{0,1:T(8,128)(4,1)} %compare_and_fusion, bf16[128,8,128]{0,2,1:T(8,128)(2,1)} %bitcast.573, bf16[2048,512]{1,0:T(8,128)(2,1)S(1)} %bitcast.535), kind=kOutput, calls=%fused_computation.278 | convolution fusion | flops 545261568 | bytes 9441280 | tf_op jit(solution)/shard_map/sub | solution.py:29
  86.0 7.0 %fusion.244 = (f32[8,128]{1,0:T(8,128)S(1)}, f32[8,128,2048]{1,2,0:T(8,128)}) fusion(pred[128,2048]{0,1:T(8,128)(4,1)} %compare_and_fusion, bf16[128,8,128]{0,2,1:T(8,128)(2,1)} %bitcast.569, bf16[2048,512]{1,0:T(8,128)(2,1)S(1)} %bitcast.536), kind=kOutput, calls=%fused_computation.281 | convolution fusion | flops 545261568 | bytes 9441280 | tf_op jit(solution)/shard_map/sub | solution.py:29
  93.0 6.0 %fusion.138 = f32[2048,128]{0,1:T(8,128)} fusion(bf16[128,8,128]{0,2,1:T(8,128)(2,1)} %bitcast.561, f32[8,128,2048]{1,2,0:T(8,128)} %get-tuple-element.45, f32[8,128]{1,0:T(8,128)S(1)} %get-tuple-element.44), kind=kOutput, calls=%fused_computation.169 | convolution fusion | flops 541065216 | bytes 9703424 | tf_op jit(solution)/shard_map/htk,thd->kd/dot_general | solution.py:41
  99.0 6.0 %fusion.126 = f32[2048,128]{0,1:T(8,128)} fusion(bf16[128,8,128]{0,2,1:T(8,128)(2,1)S(1)} %bitcast.555, f32[8,128,2048]{1,2,0:T(8,128)} %get-tuple-element.37, f32[8,128]{1,0:T(8,128)S(1)} %get-tuple-element.36), kind=kOutput, calls=%fused_computation.165 | convolution fusion | flops 541065216 | bytes 9703424 | tf_op jit(solution)/shard_map/htk,thd->kd/dot_general | solution.py:41
  112.9 7.4 %fusion.240 = (f32[8,128]{1,0:T(8,128)S(1)}, f32[8,128,2048]{1,2,0:T(8,128)}) fusion(pred[128,2048]{0,1:T(8,128)(4,1)} %compare_and_fusion, bf16[128,8,128]{0,2,1:T(8,128)(2,1)} %bitcast.563, bf16[2048,512]{1,0:T(8,128)(2,1)S(1)} %bitcast.537), kind=kOutput, calls=%fused_computation.277 | convolution fusion | flops 545261568 | bytes 9441280 | tf_op jit(solution)/shard_map/sub | solution.py:29
  120.3 7.0 %fusion.237 = (f32[8,128]{1,0:T(8,128)S(1)}, f32[8,128,2048]{1,2,0:T(8,128)}) fusion(pred[128,2048]{0,1:T(8,128)(4,1)} %compare_and_fusion, bf16[128,8,128]{0,2,1:T(8,128)(2,1)} %bitcast.565, bf16[2048,512]{1,0:T(8,128)(2,1)S(1)} %bitcast.538), kind=kOutput, calls=%fused_computation.274 | convolution fusion | flops 545261568 | bytes 9441280 | tf_op jit(solution)/shard_map/sub | solution.py:29
  127.3 6.0 %fusion.132 = f32[2048,128]{0,1:T(8,128)} fusion(bf16[128,8,128]{0,2,1:T(8,128)(2,1)S(1)} %bitcast.553, f32[8,128,2048]{1,2,0:T(8,128)} %get-tuple-element.49, f32[8,128]{1,0:T(8,128)S(1)} %get-tuple-element.48), kind=kOutput, calls=%fused_computation.167 | convolution fusion | flops 541065216 | bytes 9703424 | tf_op jit(solution)/shard_map/htk,thd->kd/dot_general | solution.py:41
  138.6 5.5 %fusion.172 = f32[2048,128,8]{1,0,2:T(8,128)} fusion(bf16[128,8,128]{0,2,1:T(8,128)(2,1)S(1)} %bitcast.562, bf16[2048,512]{1,0:T(8,128)(2,1)} %all-gather.2.cloned.1.call-done), kind=kOutput, calls=%fused_computation.202 | convolution fusion | flops 536870912 | bytes 9175040 | tf_op jit(solution)/shard_map/thd,kd->htk/dot_general | solution.py:32
  144.1 14.3 %fusion.113 = f32[2048,128]{0,1:T(8,128)} fusion(bf16[128,8,128]{0,2,1:T(8,128)(2,1)} %bitcast.578, f32[2048,128,8]{1,0,2:T(8,128)} %fusion.172, f32[8,128,2048]{1,2,0:T(8,128)} %get-tuple-element.45, f32[8,128]{1,0:T(8,128)S(1)} %get-tuple-element.44), kind=kOutput, calls=%fused_computation.156 | convolution fusion | flops 551554048 | bytes 18092032 | tf_op jit(solution)/shard_map/htk,thd->kd/dot_general | solution.py:38
  162.9 14.3 %fusion.117 = f32[2048,128]{0,1:T(8,128)} fusion(bf16[128,8,128]{0,2,1:T(8,128)(2,1)} %bitcast.572, f32[2048,128,8]{1,0,2:T(8,128)} %fusion.173, f32[8,128,2048]{1,2,0:T(8,128)} %get-tuple-element.37, f32[8,128]{1,0:T(8,128)S(1)} %get-tuple-element.36), kind=kOutput, calls=%fused_computation.160 | convolution fusion | flops 551554048 | bytes 18092032 | tf_op jit(solution)/shard_map/htk,thd->kd/dot_general | solution.py:38
  181.6 14.2 %fusion.114 = f32[2048,128]{0,1:T(8,128)} fusion(bf16[128,8,128]{0,2,1:T(8,128)(2,1)} %bitcast.576, f32[2048,128,8]{1,0,2:T(8,128)} %fusion.170, f32[8,128,2048]{1,2,0:T(8,128)} %get-tuple-element.47, f32[8,128]{1,0:T(8,128)S(1)} %get-tuple-element.46), kind=kOutput, calls=%fused_computation.157 | convolution fusion | flops 551554048 | bytes 18092032 | tf_op jit(solution)/shard_map/htk,thd->kd/dot_general | solution.py:38
  200.3 14.0 %fusion.118 = f32[2048,128]{0,1:T(8,128)} fusion(bf16[128,8,128]{0,2,1:T(8,128)(2,1)S(1)} %bitcast.568, f32[2048,128,8]{1,0,2:T(8,128)} %fusion.171, f32[8,128,2048]{1,2,0:T(8,128)} %get-tuple-element.39, f32[8,128]{1,0:T(8,128)S(1)} %get-tuple-element.38), kind=kOutput, calls=%fused_computation.161 | convolution fusion | flops 551554048 | bytes 18092032 | tf_op jit(solution)/shard_map/htk,thd->kd/dot_general | solution.py:38
  214.4 4.5 %fusion.174 = f32[2048,128,8]{1,0,2:T(8,128)} fusion(bf16[128,8,128]{0,2,1:T(8,128)(2,1)S(1)} %bitcast.558, bf16[2048,512]{1,0:T(8,128)(2,1)S(1)} %copy-done), kind=kOutput, calls=%fused_computation.204 | convolution fusion | flops 536870912 | bytes 9175040 | tf_op jit(solution)/shard_map/thd,kd->htk/dot_general | solution.py:32
  218.9 14.5 %fusion.112 = f32[2048,128]{0,1:T(8,128)} fusion(bf16[128,8,128]{0,2,1:T(8,128)(2,1)S(1)} %bitcast.574, f32[2048,128,8]{1,0,2:T(8,128)} %fusion.174, f32[8,128,2048]{1,2,0:T(8,128)} %get-tuple-element.43, f32[8,128]{1,0:T(8,128)S(1)} %get-tuple-element.42), kind=kOutput, calls=%fused_computation.155 | convolution fusion | flops 551554048 | bytes 18092032 | tf_op jit(solution)/shard_map/htk,thd->kd/dot_general | solution.py:38
  237.9 14.6 %fusion.115 = f32[2048,128]{0,1:T(8,128)} fusion(bf16[128,8,128]{0,2,1:T(8,128)(2,1)S(1)} %bitcast.570, f32[2048,128,8]{1,0,2:T(8,128)} %fusion.168, f32[8,128,2048]{1,2,0:T(8,128)} %get-tuple-element.49, f32[8,128]{1,0:T(8,128)S(1)} %get-tuple-element.48), kind=kOutput, calls=%fused_computation.158 | convolution fusion | flops 551554048 | bytes 18092032 | tf_op jit(solution)/shard_map/htk,thd->kd/dot_general | solution.py:38
  256.9 14.0 %fusion.119 = f32[2048,128]{0,1:T(8,128)} fusion(bf16[128,8,128]{0,2,1:T(8,128)(2,1)S(1)} %bitcast.564, f32[2048,128,8]{1,0,2:T(8,128)} %fusion.169, f32[8,128,2048]{1,2,0:T(8,128)} %get-tuple-element.41, f32[8,128]{1,0:T(8,128)S(1)} %get-tuple-element.40), kind=kOutput, calls=%fused_computation.162 | convolution fusion | flops 551554048 | bytes 18092032 | tf_op jit(solution)/shard_map/htk,thd->kd/dot_general | solution.py:38
  275.4 14.5 %fusion.116 = f32[2048,128]{0,1:T(8,128)} fusion(bf16[128,8,128]{0,2,1:T(8,128)(2,1)S(1)} %bitcast.566, f32[2048,128,8]{1,0,2:T(8,128)} %fusion.175, f32[8,128,2048]{1,2,0:T(8,128)} %get-tuple-element.35, f32[8,128]{1,0:T(8,128)S(1)} %get-tuple-element.34), kind=kOutput, calls=%fused_computation.159 | convolution fusion | flops 551554048 | bytes 18092032 | tf_op jit(solution)/shard_map/htk,thd->kd/dot_general | solution.py:38
  289.8 8.3 %maximum_add_fusion = (f32[2048,512]{0,1:T(8,128)S(1)}, f32[2048,512]{0,1:T(8,128)}) fusion(f32[2048,128]{0,1:T(8,128)} %fusion.116, f32[2048,128]{0,1:T(8,128)} %fusion.117, f32[2048,128]{0,1:T(8,128)} %fusion.118, f32[2048,128]{0,1:T(8,128)} %fusion.119, f32[2048,128]{0,1:T(8,128)} %fusion.112, f32[2048,128]{0,1:T(8,128)} %fusion.113, ...), kind=kLoop, calls=%fused_computation.81 | loop fusion | flops 14680064 | bytes 25165824 | tf_op jit(solution)/shard_map/add | solution.py:96
  298.1 6.5 %pad_maximum_fusion = f32[2048,1024]{0,1:T(8,128)} fusion(f32[2048,512]{0,1:T(8,128)} %get-tuple-element.51, f32[2048,512]{0,1:T(8,128)S(1)} %get-tuple-element.50), kind=kLoop, calls=%fused_computation.16 | loop fusion | flops 2097152 | bytes 16777216 | tf_op jit(solution)/shard_map/concatenate | solution.py:96
  306.2 13.7 %fusion.145 = bf16[8,128,128]{1,2,0:T(8,128)(2,1)S(1)} fusion(f32[2048,128,8]{1,0,2:T(8,128)} %fusion.172, bf16[2048,512]{1,0:T(8,128)(2,1)S(1)} %bitcast.539, f32[8,128,2048]{1,2,0:T(8,128)} %get-tuple-element.45, f32[8,128]{1,0:T(8,128)S(1)} %get-tuple-element.44), kind=kOutput, calls=%fused_computation.172 | convolution fusion | flops 551685120 | bytes 34349056 | tf_op jit(solution)/shard_map/htk,kd->thd/dot_general | solution.py:35
  320.1 15.7 %fusion.149 = bf16[8,128,128]{1,2,0:T(8,128)(2,1)S(1)} fusion(f32[2048,128,8]{1,0,2:T(8,128)} %fusion.173, bf16[2048,512]{1,0:T(8,128)(2,1)S(1)} %bitcast.540, f32[8,128,2048]{1,2,0:T(8,128)} %get-tuple-element.37, f32[8,128]{1,0:T(8,128)S(1)} %get-tuple-element.36), kind=kOutput, calls=%fused_computation.176 | convolution fusion | flops 551685120 | bytes 34349056 | tf_op jit(solution)/shard_map/htk,kd->thd/dot_general | solution.py:35
  336.0 13.8 %fusion.146 = bf16[8,128,128]{1,2,0:T(8,128)(2,1)S(1)} fusion(f32[2048,128,8]{1,0,2:T(8,128)} %fusion.170, bf16[2048,512]{1,0:T(8,128)(2,1)S(1)} %bitcast.541, f32[8,128,2048]{1,2,0:T(8,128)} %get-tuple-element.47, f32[8,128]{1,0:T(8,128)S(1)} %get-tuple-element.46), kind=kOutput, calls=%fused_computation.173 | convolution fusion | flops 551685120 | bytes 34349056 | tf_op jit(solution)/shard_map/htk,kd->thd/dot_general | solution.py:35
  349.9 13.4 %fusion.150 = bf16[8,128,128]{1,2,0:T(8,128)(2,1)S(1)} fusion(f32[2048,128,8]{1,0,2:T(8,128)} %fusion.171, bf16[2048,512]{1,0:T(8,128)(2,1)S(1)} %bitcast.542, f32[8,128,2048]{1,2,0:T(8,128)} %get-tuple-element.39, f32[8,128]{1,0:T(8,128)S(1)} %get-tuple-element.38), kind=kOutput, calls=%fused_computation.177 | convolution fusion | flops 551685120 | bytes 34349056 | tf_op jit(solution)/shard_map/htk,kd->thd/dot_general | solution.py:35
  363.5 14.4 %fusion.144 = bf16[8,128,128]{1,2,0:T(8,128)(2,1)} fusion(f32[2048,128,8]{1,0,2:T(8,128)} %fusion.174, bf16[2048,512]{1,0:T(8,128)(2,1)S(1)} %bitcast.543, f32[8,128,2048]{1,2,0:T(8,128)} %get-tuple-element.43, f32[8,128]{1,0:T(8,128)S(1)} %get-tuple-element.42), kind=kOutput, calls=%fused_computation.171 | convolution fusion | flops 551685120 | bytes 34349056 | tf_op jit(solution)/shard_map/htk,kd->thd/dot_general | solution.py:35
  379.0 13.7 %fusion.147 = bf16[8,128,128]{1,2,0:T(8,128)(2,1)} fusion(f32[2048,128,8]{1,0,2:T(8,128)} %fusion.168, bf16[2048,512]{1,0:T(8,128)(2,1)S(1)} %bitcast.544, f32[8,128,2048]{1,2,0:T(8,128)} %get-tuple-element.49, f32[8,128]{1,0:T(8,128)S(1)} %get-tuple-element.48), kind=kOutput, calls=%fused_computation.174 | convolution fusion | flops 551685120 | bytes 34349056 | tf_op jit(solution)/shard_map/htk,kd->thd/dot_general | solution.py:35
  394.5 14.0 %fusion.151 = bf16[8,128,128]{1,2,0:T(8,128)(2,1)} fusion(f32[2048,128,8]{1,0,2:T(8,128)} %fusion.169, bf16[2048,512]{1,0:T(8,128)(2,1)S(1)} %bitcast.545, f32[8,128,2048]{1,2,0:T(8,128)} %get-tuple-element.41, f32[8,128]{1,0:T(8,128)S(1)} %get-tuple-element.40), kind=kOutput, calls=%fused_computation.178 | convolution fusion | flops 551685120 | bytes 34349056 | tf_op jit(solution)/shard_map/htk,kd->thd/dot_general | solution.py:35
  410.3 13.7 %fusion.148 = bf16[8,128,128]{1,2,0:T(8,128)(2,1)} fusion(f32[2048,128,8]{1,0,2:T(8,128)} %fusion.175, bf16[2048,512]{1,0:T(8,128)(2,1)S(1)} %bitcast.546, f32[8,128,2048]{1,2,0:T(8,128)} %get-tuple-element.35, f32[8,128]{1,0:T(8,128)S(1)} %get-tuple-element.34), kind=kOutput, calls=%fused_computation.175 | convolution fusion | flops 551685120 | bytes 34349056 | tf_op jit(solution)/shard_map/htk,kd->thd/dot_general | solution.py:35
  (114 shorter events, 86.5 us)
Async XLA Ops:
  7.2 23.0 %copy-start.10 = (bf16[128,4096]{1,0:T(8,128)(2,1)S(1)}, bf16[128,4096]{1,0:T(8,128)(2,1)}, u32[]{:S(2)}) copy-start(bf16[128,4096]{1,0:T(8,128)(2,1)} %param.9) | copy-start | bytes 3145732
  7.2 131.4 %all-gather.2.cloned.1.call-start = ((), (), s32[]{:S(2)}) async-start(), calls=%async_computation.2 | async-start | bytes 2228224 | tf_op jit(solution)/shard_map/all_gather | solution.py:76
  10.4 39.9 %all-to-all-start = ((bf16[16,128,512]{2,1,0:T(8,128)(2,1)}), bf16[16,128,512]{2,1,0:T(8,128)(2,1)S(1)}, u32[]{:S(2)}, u32[]{:S(2)}) async-start(bf16[16,128,512]{2,1,0:T(8,128)(2,1)} %stack.2), calls=%async_computation | async-start | bytes 4194304 | tf_op jit(solution)/shard_map/all_to_all | solution.py:72
  19.8 407.8 %reduce-scatter.2.cloned.1.call-start = ((), (), s32[]{:S(2)}) async-start(), calls=%async_computation.3 | async-start | bytes 8912896 | tf_op jit(solution)/shard_map/reduce_scatter | solution.py:97
  50.3 70.0 %copy-start.1 = (bf16[16,128,512]{2,1,0:T(8,128)(2,1)}, bf16[16,128,512]{2,1,0:T(8,128)(2,1)S(1)}, u32[]{:S(2)}) copy-start(bf16[16,128,512]{2,1,0:T(8,128)(2,1)S(1)} %all-to-all-done) | copy-start | bytes 6291460
  93.0 12.1 %slice-start.6 = ((s8[8388608]{0:T(1024)(128)(4,1)}), s8[4194304]{0:T(1024)(128)(4,1)S(1)}, s32[]{:S(2)}) async-start(s8[8388608]{0:T(1024)(128)(4,1)} %bitcast.595), calls=%async_computation.10 | async-start | bytes 8388608
  99.0 6.0 %slice-start.7 = ((s8[8388608]{0:T(1024)(128)(4,1)}), s8[4194304]{0:T(1024)(128)(4,1)S(1)}, s32[]{:S(2)}) async-start(s8[8388608]{0:T(1024)(128)(4,1)} %bitcast.595), calls=%async_computation.11 | async-start | bytes 8388608
  99.0 6.0 %copy-start.5 = (bf16[128,1024]{0,1:T(8,128)(2,1)S(1)}, bf16[128,1024]{0,1:T(8,128)(2,1)}, u32[]{:S(2)}) copy-start(bf16[128,1024]{0,1:T(8,128)(2,1)} %copy.285) | copy-start | bytes 786436
  99.0 8.6 %slice-start.4 = ((s8[8388608]{0:T(1024)(128)(4,1)}), s8[4194304]{0:T(1024)(128)(4,1)S(1)}, s32[]{:S(2)}) async-start(s8[8388608]{0:T(1024)(128)(4,1)} %bitcast.593), calls=%async_computation.8 | async-start | bytes 8388608
  105.1 2.6 slice-start.5
  105.1 5.1 %slice-start = ((s8[8388608]{0:T(1024)(128)(4,1)}), s8[4194304]{0:T(1024)(128)(4,1)S(1)}, s32[]{:S(2)}) async-start(s8[8388608]{0:T(1024)(128)(4,1)} %bitcast.589), calls=%async_computation.4 | async-start | bytes 8388608
  107.6 2.5 copy-start.3
  107.6 2.8 slice-start.1
  127.3 6.1 %copy-start.16 = (f32[8,128,2048]{1,2,0:T(8,128)S(1)}, f32[8,128,2048]{1,2,0:T(8,128)}, u32[]{:S(2)}) copy-start(f32[8,128,2048]{1,2,0:T(8,128)} %get-tuple-element.41) | copy-start | bytes 25165828
  127.3 8.5 %slice-start.2 = ((s8[8388608]{0:T(1024)(128)(4,1)}), s8[4194304]{0:T(1024)(128)(4,1)S(1)}, s32[]{:S(2)}) async-start(s8[8388608]{0:T(1024)(128)(4,1)} %bitcast.591), calls=%async_computation.6 | async-start | bytes 8388608
  133.4 2.7 slice-start.3
  136.1 2.5 copy-start.7
  144.1 14.3 %copy-start = (bf16[2048,512]{1,0:T(8,128)(2,1)S(1)}, bf16[2048,512]{1,0:T(8,128)(2,1)}, u32[]{:S(2)}) copy-start(bf16[2048,512]{1,0:T(8,128)(2,1)} %all-gather.2.cloned.1.call-done) | copy-start | bytes 6291460
  162.9 14.3 %copy-start.6 = (bf16[128,1024]{0,1:T(8,128)(2,1)S(1)}, bf16[128,1024]{0,1:T(8,128)(2,1)}, u32[]{:S(2)}) copy-start(bf16[128,1024]{0,1:T(8,128)(2,1)} %copy.285) | copy-start | bytes 786436
  195.8 4.5 %copy-start.13 = (bf16[128,1024]{0,1:T(8,128)(2,1)S(1)}, bf16[128,1024]{0,1:T(8,128)(2,1)}, u32[]{:S(2)}) copy-start(bf16[128,1024]{0,1:T(8,128)(2,1)} %copy.276) | copy-start | bytes 786436
  200.3 14.0 %copy-start.4 = (bf16[128,1024]{0,1:T(8,128)(2,1)S(1)}, bf16[128,1024]{0,1:T(8,128)(2,1)}, u32[]{:S(2)}) copy-start(bf16[128,1024]{0,1:T(8,128)(2,1)} %copy.289) | copy-start | bytes 786436
  214.3 4.5 %copy-start.15 = (bf16[128,1024]{0,1:T(8,128)(2,1)S(1)}, bf16[128,1024]{0,1:T(8,128)(2,1)}, u32[]{:S(2)}) copy-start(bf16[128,1024]{0,1:T(8,128)(2,1)} %copy.288) | copy-start | bytes 786436
  233.4 4.4 %copy-start.14 = (bf16[128,1024]{0,1:T(8,128)(2,1)S(1)}, bf16[128,1024]{0,1:T(8,128)(2,1)}, u32[]{:S(2)}) copy-start(bf16[128,1024]{0,1:T(8,128)(2,1)} %copy.282) | copy-start | bytes 786436
  252.4 4.5 %copy-start.11 = (bf16[128,1024]{0,1:T(8,128)(2,1)S(1)}, bf16[128,1024]{0,1:T(8,128)(2,1)}, u32[]{:S(2)}) copy-start(bf16[128,1024]{0,1:T(8,128)(2,1)} %copy.274) | copy-start | bytes 786436
  270.9 4.4 %copy-start.12 = (bf16[128,1024]{0,1:T(8,128)(2,1)S(1)}, bf16[128,1024]{0,1:T(8,128)(2,1)}, u32[]{:S(2)}) copy-start(bf16[128,1024]{0,1:T(8,128)(2,1)} %copy.280) | copy-start | bytes 786436
  275.4 14.5 %copy-start.8 = (f32[2048,128]{0,1:T(8,128)S(1)}, f32[2048,128]{0,1:T(8,128)}, u32[]{:S(2)}) copy-start(f32[2048,128]{0,1:T(8,128)} %fusion.138) | copy-start | bytes 3145732
  275.4 14.5 %copy-start.9 = (f32[2048,128]{0,1:T(8,128)S(1)}, f32[2048,128]{0,1:T(8,128)}, u32[]{:S(2)}) copy-start(f32[2048,128]{0,1:T(8,128)} %fusion.126) | copy-start | bytes 3145732
  304.6 1.6 copy-start.2
Sparse Core Ops, SparseCore 0:
  10.5 62.3 all-gather.1
  304.8 102.3 reduce-scatter.1
